TPU v7x, 512 devices: a whole 4x8x8 slice. The times are simulated.
512 devices in a mesh: row: 32 (over x, z_hi, core), col: 16 (over z_lo, y).
Axes of the slice: x: 4, y: 8, z: 8 (z_hi: 4, z_lo: 2; z = z_hi * 2 + z_lo), core: 2. Of those that a mesh axis runs over, the one named last changes fastest.
Arguments:
- tokens: bfloat16 [1152, 8192], P('row', 'col'), may hold values from -6 to 6
- gate_weight: bfloat16 [8192, 28672], P('col', 'row'), may hold values from -0.0625 to 0.0625
- up_weight: bfloat16 [8192, 28672], P('col', 'row'), may hold values from -0.0625 to 0.0625
- down_weight: bfloat16 [28672, 8192], P('row', 'col'), may hold values from -0.03125 to 0.03125
Outputs:
- mixed: bfloat16 [1152, 8192], P('row', 'col')
All inputs are finite; a program needn't handle non-finite values.
Results may differ from a plain program's by a relative error of at most 0.005.
Values may be sent and summed in bfloat16 or wider, within the bound.
A program may use at most 64 MiB of HBM per device.

v0:
```python
import jax
import jax.numpy as jnp
from jax import lax
from jax.sharding import PartitionSpec as P


def per_device(tokens, gate_weight, up_weight, down_weight):
    units = gate_weight.shape[1]
    both_weight = jnp.concatenate([gate_weight, up_weight], axis=1)
    terms = jnp.dot(
        lax.all_gather(tokens, "row", axis=0, tiled=True),
        both_weight,
        preferred_element_type=jnp.float32,
    )
    summed = lax.psum(terms, "col")
    hidden = (jax.nn.silu(summed[:, :units]) * summed[:, units:]).astype(jnp.bfloat16)
    mixed = lax.psum_scatter(
        jnp.dot(hidden, down_weight, preferred_element_type=jnp.float32),
        "row",
        scatter_dimension=0,
        tiled=True,
    )
    return mixed.astype(jnp.bfloat16)


def solution(mesh):
    in_specs = (P("row", "col"), P("col", "row"), P("col", "row"), P("row", "col"))
    out_specs = P("row", "col")
    return jax.shard_map(
        per_device, mesh=mesh, in_specs=in_specs, out_specs=out_specs, check_vma=False
    )
```

profile of v0, /device:TPU:23, one launch (start us, length us, event | category | flops | bytes accessed | tf_op | source)
XLA Modules:
  0.0 402.3 jit_solution(3805615868372973947)
XLA Ops:
  6.5 0.0 copy-start
  6.5 0.0 all-gather.3.cloned.1.call-start
  6.5 0.7 all-gather.3.cloned.1.call-update
  7.3 0.0 all-reduce.4.cloned.1.call-start
  7.3 65.3 %all-gather.3.cloned.1.call-done = bf16[32,36,512]{2,1,0:T(8,128)(2,1)} async-done(((bf16[1,36,512]{2,1,0:T(8,128)(2,1)}), bf16[32,36,512]{2,1,0:T(8,128)(2,1)}) %all-gather.3.cloned.1.call-update) | async-done | bytes 1179664 | tf_op jit(solution)/shard_map/all_gather | solution.py:11
  72.6 2.1 reshape.1
  74.8 7.2 %convolution_bitcast_fusion = f32[1152,1792]{0,1:T(8,128)} fusion(bf16[1152,512]{1,0:T(8,128)(2,1)S(1)} %reshape.1, bf16[512,896]{1,0:T(8,128)(2,1)} %param.6, bf16[512,896]{1,0:T(8,128)(2,1)} %param.5), kind=kOutput, calls=%fused_computation | convolution fusion | flops 2117599232 | bytes 11272192 | tf_op jit(solution)/shard_map/dot_general | solution.py:10
  82.0 0.0 all-reduce.4.cloned.1.call-update
  82.0 198.9 %all-reduce.4.cloned.1.call-done = f32[1152,1792]{0,1:T(8,128)} async-done(((f32[1152,1792]{0,1:T(8,128)}), f32[1152,1792]{0,1:T(8,128)}) %all-reduce.4.cloned.1.call-update) | async-done | bytes 8257552 | tf_op jit(solution)/shard_map/psum | solution.py:15
  280.9 0.0 copy-done
  280.9 4.9 %fusion.2 = f32[1152,512]{1,0:T(8,128)S(1)} fusion(bf16[896,512]{1,0:T(8,128)(2,1)S(1)} %copy-done, f32[1152,1792]{0,1:T(8,128)} %all-reduce.4.cloned.1.call-done), kind=kOutput, calls=%fused_computation.3 | convolution fusion | flops 1063157760 | bytes 11534336 | tf_op jit(solution)/shard_map/dot_general | solution.py:18
  285.8 74.1 %fusion = f32[40,512]{1,0:T(8,128)S(1)} fusion(f32[1152,512]{1,0:T(8,128)S(1)} %fusion.2), kind=kCustom, calls=%all-reduce-scatter | all-reduce-scatter fusion | flops 655361 | bytes 2443264
  359.9 3.9 collective-permute-start
  363.8 10.1 %collective-permute-start.1 = (bf16[40,512]{1,0:T(8,128)(2,1)S(1)}, bf16[40,512]{1,0:T(8,128)(2,1)S(1)}, u32[]{:S(2)}, u32[]{:S(2)}) collective-permute-start(bf16[40,512]{1,0:T(8,128)(2,1)S(1)} %convert.6), channel_id=1, source_target_pairs={{0,32},{16,48},{32,64},{48,80},{64,96},{80,112},{96,128},{112,144}... | collective-permute-start | bytes 122888
  373.9 11.0 %collective-permute-start.2 = (bf16[40,512]{1,0:T(8,128)(2,1)S(1)}, bf16[40,512]{1,0:T(8,128)(2,1)S(1)}, u32[]{:S(2)}, u32[]{:S(2)}) collective-permute-start(bf16[40,512]{1,0:T(8,128)(2,1)S(1)} %convert.6), channel_id=1, source_target_pairs={{0,48},{16,64},{32,80},{48,96},{64,112},{80,128},{96,144},{112,160... | collective-permute-start | bytes 122888
  385.0 1.9 collective-permute-start.3
  386.9 1.3 dynamic-slice.4
  388.8 5.3 %collective-permute-done.3 = bf16[4,512]{1,0:T(4,128)(2,1)S(1)} collective-permute-done((bf16[4,512]{1,0:T(4,128)(2,1)S(1)}, bf16[4,512]{1,0:T(4,128)(2,1)S(1)}, u32[]{:S(2)}, u32[]{:S(2)}) %collective-permute-start.3) | collective-permute-done | bytes 4128
  394.1 0.0 collective-permute-done
  394.2 0.0 collective-permute-done.1
  394.2 0.0 collective-permute-done.2
  394.2 0.6 concatenate.4
  394.8 0.6 dynamic-slice_convert_fusion
  (2 shorter events, 0.0 us)
Async XLA Ops:
  6.5 274.4 %copy-start = (bf16[896,512]{1,0:T(8,128)(2,1)S(1)}, bf16[896,512]{1,0:T(8,128)(2,1)}, u32[]{:S(2)}) copy-start(bf16[896,512]{1,0:T(8,128)(2,1)} %param.7) | copy-start | bytes 2752516
  6.5 66.1 %all-gather.3.cloned.1.call-start = ((), (), s32[]{:S(2)}) async-start(), calls=%async_computation.1 | async-start | bytes 1351680 | tf_op jit(solution)/shard_map/all_gather | solution.py:11
  7.3 273.6 %all-reduce.4.cloned.1.call-start = ((), (), s32[]{:S(2)}) async-start(), calls=%async_computation | async-start | bytes 16515072 | tf_op jit(solution)/shard_map/psum | solution.py:15
  359.9 34.2 %collective-permute-start = (bf16[40,512]{1,0:T(8,128)(2,1)S(1)}, bf16[40,512]{1,0:T(8,128)(2,1)S(1)}, u32[]{:S(2)}, u32[]{:S(2)}) collective-permute-start(bf16[40,512]{1,0:T(8,128)(2,1)S(1)} %convert.6), channel_id=1, source_target_pairs={{0,16},{16,32},{32,48},{48,64},{64,80},{80,96},{96,112},{112,128},... | collective-permute-start | bytes 122888
  363.8 30.3 %collective-permute-start.1 = (bf16[40,512]{1,0:T(8,128)(2,1)S(1)}, bf16[40,512]{1,0:T(8,128)(2,1)S(1)}, u32[]{:S(2)}, u32[]{:S(2)}) collective-permute-start(bf16[40,512]{1,0:T(8,128)(2,1)S(1)} %convert.6), channel_id=1, source_target_pairs={{0,32},{16,48},{32,64},{48,80},{64,96},{80,112},{96,128},{112,144}... | collective-permute-start | bytes 122888
  373.9 20.2 %collective-permute-start.2 = (bf16[40,512]{1,0:T(8,128)(2,1)S(1)}, bf16[40,512]{1,0:T(8,128)(2,1)S(1)}, u32[]{:S(2)}, u32[]{:S(2)}) collective-permute-start(bf16[40,512]{1,0:T(8,128)(2,1)S(1)} %convert.6), channel_id=1, source_target_pairs={{0,48},{16,64},{32,80},{48,96},{64,112},{80,128},{96,144},{112,160... | collective-permute-start | bytes 122888
  385.0 9.2 %collective-permute-start.3 = (bf16[4,512]{1,0:T(4,128)(2,1)S(1)}, bf16[4,512]{1,0:T(4,128)(2,1)S(1)}, u32[]{:S(2)}, u32[]{:S(2)}) collective-permute-start(bf16[4,512]{1,0:T(4,128)(2,1)S(1)} %slice.10), channel_id=1, source_target_pairs={{0,64},{16,80},{32,96},{48,112},{64,128},{80,144},{96,160},{112,17... | collective-permute-start | bytes 12296
Sparse Core Ops, SparseCore 0:
  10.5 62.0 all-gather.2
  82.1 198.6 all-reduce.3
where the time goes:
time: 403 us; the launch traced here: 402 us
  waiting for transfers between devices  270 us (67%)
  blocking collectives  74.1 us (18%)
  starting transfers between devices  27 us (7%)
  between operations  14.1 us (3%)
  matrix products  12.2 us (3%)
  local copies, waits for them, and re-layouts  4.68 us (1%)
    psum x1, waiting for transfers between devices, per_device(): summed = lax.psum(terms, 'col')  199 us
    unnamed x1, blocking collectives  74.1 us
    all_gather x1, waiting for transfers between devices, per_device(): lax.all_gather(tokens, 'row', axis=0, tiled=True)  65.3 us
    unnamed x4, starting transfers between devices  27 us
  transfers between devices with their start and end apart: 6, of which 3 were waited for; matrix products, arithmetic and copies ran while one was open for 0% of the time, Pallas kernels for 0%

commit v1 on v0

v1 whole, which is shorter than its diff:
```python
import functools

import jax
import jax.numpy as jnp
from jax import lax
from jax.experimental import pallas as pl
from jax.experimental.pallas import tpu as pltpu
from jax.sharding import PartitionSpec as P

F32, BF16 = jnp.float32, jnp.bfloat16
NX, NY, NZ = 4, 8, 8
TOK = 36
BLK = 144
GRP = 512
NF = 7
NCH = 4
ZTYPE = BF16


def device(x, y, z, c):
    return {"row": (x * 4 + z // 2) * 2 + c, "col": lax.rem(z, 2) * 8 + y}


def kernel(
    tok, gate, up, down, out,
    fs, tz, xf, tx, wgu, dw, sl, slf, ss, ssf, rl, rlf, rs, rsf, hb, xs, xr, xo, zsf, zs, zr,
    tz_s, tz_r, tx_s, tx_r, wl, wz_s, wz_r, wo_s, wo_r, wf_s, wf_r, dl, dz_s, dz_r, do_s, do_r, df_s, df_r,
    rl_s, rl_r, rs_s, rs_r, gl_s, gl_r, gs_s, gs_r, xx_s, xx_r, zz_s, zz_r,
):
    row, col = lax.axis_index("row"), lax.axis_index("col")
    x, zh, c = row // 8, lax.rem(row // 2, 4), lax.rem(row, 2)
    zl, y = col // 8, lax.rem(col, 8)
    z = zh * 2 + zl
    primary = c == zl

    def at(dx=0, dy=0, dz=0):
        return device(lax.rem(x + dx + NX, NX), lax.rem(y + dy + NY, NY), lax.rem(z + dz + NZ, NZ), c)

    other_core = device(x, y, z, 1 - c)
    z_partner = device(x, y, zh * 2 + (1 - zl), c)
    xoff = lambda i: jnp.where(i == 0, 1, jnp.where(i == 1, -1, jnp.where(i == 2, 2, 0)))

    def copy(src, dst, send, recv, where):
        return pltpu.make_async_remote_copy(
            src_ref=src, dst_ref=dst, send_sem=send, recv_sem=recv,
            device_id=where, device_id_type=pl.DeviceIdType.MESH,
        )

    mine = pl.ds(pl.multiple_of(zl * GRP, GRP), GRP)
    theirs = pl.ds(pl.multiple_of((1 - zl) * GRP, GRP), GRP)
    cols = lambda f: pl.ds(pl.multiple_of(f * 128, 128), 128)

    bar = pltpu.get_barrier_semaphore()
    peers = [at(dz=k) for k in range(1, NZ)] + [at(dx=k) for k in range(1, NX)]
    peers += [at(dy=1), at(dy=-1), other_core]
    for p in peers:
        pl.semaphore_signal(bar, inc=1, device_id=p, device_id_type=pl.DeviceIdType.MESH)

    @pl.when(primary)
    def _():
        for f in range(NF):
            pltpu.make_async_copy(gate.at[:, cols(f)], wgu.at[f, mine, pl.ds(0, 128)], wl).start()
            pltpu.make_async_copy(up.at[:, cols(f)], wgu.at[f, mine, pl.ds(128, 128)], wl).start()
        pltpu.make_async_copy(down, dw.at[zl], dl).start()

    t = tok[...].astype(F32)
    for k in range(4):
        fs[k * TOK:(k + 1) * TOK, :] = t[:, k * 128:(k + 1) * 128]
    tz[z] = fs[...].astype(BF16)

    pl.semaphore_wait(bar, len(peers))

    def tz_copy(k):
        return copy(tz.at[z], tz.at[z], tz_s.at[k], tz_r.at[k], at(dz=k))

    for k in (4, 3, 5, 2, 6, 1, 7):
        tz_copy(k).start()

    order = (4, -3, 3, -2, 2, -1, 1, 0)

    def block(offset):
        return lax.rem(y + offset + NY, NY)

    def weight_z(f):
        return (
            copy(gate.at[:, cols(f)], wgu.at[f, mine, pl.ds(0, 128)], wz_s.at[f], wz_r.at[f], z_partner),
            copy(up.at[:, cols(f)], wgu.at[f, mine, pl.ds(128, 128)], wz_s.at[f], wz_r.at[f], z_partner),
        )

    def weight_own(f):
        return (
            copy(gate.at[:, cols(f)], wgu.at[f, mine, pl.ds(0, 128)], wo_s, wo_r, other_core),
            copy(up.at[:, cols(f)], wgu.at[f, mine, pl.ds(128, 128)], wo_s, wo_r, other_core),
        )

    def weight_fwd(f):
        return copy(wgu.at[f, theirs], wgu.at[f, theirs], wf_s.at[f], wf_r.at[f], other_core)

    down_z = copy(down, dw.at[zl], dz_s, dz_r, z_partner)
    down_own = copy(down, dw.at[zl], do_s, do_r, other_core)
    down_fwd = copy(dw.at[1 - zl], dw.at[1 - zl], df_s, df_r, other_core)
    half_all = wgu.at[:, mine]

    @pl.when(jnp.logical_not(primary))
    def _():
        for o in order:
            f = block(o)

            @pl.when(f != NF)
            def _():
                for d in weight_z(f):
                    d.start()
        down_z.start()

    @pl.when(primary)
    def _():
        for f in range(NF):
            for d in weight_own(f):
                d.start()
        down_own.start()

    for k in range(1, NZ):
        pass
    for k in range(1, NZ):
        src = lax.rem(z - k + NZ, NZ)
        copy(tz.at[src], tz.at[src], tz_s.at[k], tz_r.at[k], at(dz=k)).wait_recv()
    for p in range(NZ):
        fs[...] = tz[p].astype(F32)
        for k in range(4):
            lanes = (p % 2) * GRP + k * 128
            xf[(p // 2) * TOK:(p // 2 + 1) * TOK, lanes:lanes + 128] = fs[k * TOK:(k + 1) * TOK, :]
    tx[3] = xf[...].astype(BF16)

    def tx_copy(i):
        return copy(tx.at[3], tx.at[i], tx_s.at[i], tx_r.at[i], at(dx=-(1, -1, 2)[i]))

    for i in range(3):
        tx_copy(i).start()

    @pl.when(primary)
    def _():
        pltpu.make_async_copy(half_all, half_all, wl).wait()

    @pl.when(jnp.logical_not(primary))
    def _():
        copy(half_all, wgu.at[:, theirs], wo_s, wo_r, other_core).wait_recv()

    def turn(i):
        return 1 - 2 * lax.rem(i, 2)

    def product(i, f):
        acc = jnp.dot(tx[i], wgu[f], preferred_element_type=F32)
        return jnp.concatenate([acc[:, :128], acc[:, 128:]], axis=0)

    def take_weights(i, f):
        @pl.when(i == 0)
        def _():
            @pl.when(primary)
            def _():
                copy(wgu.at[f, mine], wgu.at[f, theirs], wz_s.at[f], wz_r.at[f], z_partner).wait_recv()
                weight_fwd(f).start()

            @pl.when(jnp.logical_not(primary))
            def _():
                copy(wgu.at[f, mine], wgu.at[f, mine], wf_s.at[f], wf_r.at[f], other_core).wait_recv()

    def long_copy(i, s):
        to = at(dy=turn(i))
        if s < 3:
            return copy(sl.at[i, s], rl.at[i, s], rl_s.at[i, s], rl_r.at[i, s], to)
        return copy(slf.at[i], rlf.at[i], rl_s.at[i, s], rl_r.at[i, s], to)

    def short_copy(i, s):
        to = at(dy=-turn(i))
        if s < 2:
            return copy(ss.at[i, s], rs.at[i, s], rs_s.at[i, s], rs_r.at[i, s], to)
        return copy(ssf.at[i], rsf.at[i], rs_s.at[i, s], rs_r.at[i, s], to)

    def long_block(i, s):
        return block(turn(i) * (4 - s))

    def short_block(i, s):
        return block(-turn(i) * (3 - s))

    def reduce_step(i, s):
        f = long_block(i, s)

        @pl.when(f != NF)
        def _():
            take_weights(i, f)
            v = product(i, f)
            if s > 0:
                long_copy(i, s - 1).wait_recv()
                v = v + rl[i, s - 1].astype(F32)
            if s < 3:
                sl[i, s] = v.astype(BF16)
            else:
                slf[i] = v
            long_copy(i, s).start()

        if s == 3:
            return
        f2 = short_block(i, s)

        @pl.when(f2 != NF)
        def _():
            take_weights(i, f2)
            v = product(i, f2)
            if s > 0:
                short_copy(i, s - 1).wait_recv()
                v = v + rs[i, s - 1].astype(F32)
            if s < 2:
                ss[i, s] = v.astype(BF16)
            else:
                ssf[i] = v
            short_copy(i, s).start()

    def gather_long(i, s, f):
        return copy(hb.at[i, f], hb.at[i, f], gl_s.at[i, s], gl_r.at[i, s], at(dy=turn(i)))

    def gather_short(i, s, f):
        return copy(hb.at[i, f], hb.at[i, f], gs_s.at[i, s], gs_r.at[i, s], at(dy=-turn(i)))

    def finish(i):
        @pl.when(y != NF)
        def _():
            take_weights(i, y)
            v = product(i, y)
            long_copy(i, 3).wait_recv()
            short_copy(i, 2).wait_recv()
            v = v + rlf[i] + rsf[i]
            g, u = v[:BLK], v[BLK:]
            hb[i, y] = (g / (1.0 + jnp.exp(-g)) * u).astype(BF16)
            gather_long(i, 0, y).start()
            gather_short(i, 0, y).start()

    def gather_step(i, s):
        f = block(-turn(i) * s)

        @pl.when(f != NF)
        def _():
            gather_long(i, s - 1, f).wait_recv()
            gather_long(i, s, f).start()

        if s == 3:
            return
        f2 = block(turn(i) * s)

        @pl.when(f2 != NF)
        def _():
            gather_short(i, s - 1, f2).wait_recv()
            gather_short(i, s, f2).start()

    def x_copy(i):
        return copy(xs.at[i], xr.at[i], xx_s.at[i], xx_r.at[i], at(dx=xoff(i)))

    def project(i):
        f = block(-turn(i) * 4)

        @pl.when(f != NF)
        def _():
            gather_long(i, 3, f).wait_recv()

        f2 = block(turn(i) * 3)

        @pl.when(f2 != NF)
        def _():
            gather_short(i, 2, f2).wait_recv()

        f3 = block(turn(i) * 3)

        @pl.when(i == 0)
        def _():
            @pl.when(primary)
            def _():
                pltpu.make_async_copy(down, dw.at[zl], dl).wait()
                copy(down, dw.at[1 - zl], dz_s, dz_r, z_partner).wait_recv()
                down_fwd.start()

            @pl.when(jnp.logical_not(primary))
            def _():
                copy(down, dw.at[zl], do_s, do_r, other_core).wait_recv()
                copy(down, dw.at[1 - zl], df_s, df_r, other_core).wait_recv()

        h = jnp.concatenate([hb[i, f] for f in range(NF)], axis=1)
        for half in range(2):
            v = jnp.dot(h, dw[half], preferred_element_type=F32)
            lanes = slice(half * GRP, (half + 1) * GRP)

            @pl.when(i < 3)
            def _():
                xs[jnp.minimum(i, 2), :, lanes] = v.astype(BF16)

            @pl.when(i == 3)
            def _():
                xo[:, lanes] = v

        @pl.when(i < 3)
        def _():
            x_copy(jnp.minimum(i, 2)).start()

    stages = [functools.partial(reduce_step, s=s) for s in range(4)]
    stages += [finish] + [functools.partial(gather_step, s=s) for s in (1, 2, 3)] + [project]

    def slot(t, carry):
        for s in reversed(range(len(stages))):
            i = t - s

            @pl.when(jnp.logical_and(i >= 0, i < NCH))
            def _():
                @pl.when(jnp.logical_and(s == 0, jnp.logical_and(i >= 0, i < 3)))
                def _():
                    j = jnp.minimum(i, 2)
                    copy(tx.at[3], tx.at[j], tx_s.at[j], tx_r.at[j], at(dx=-xoff(j))).wait_recv()

                stages[s](i)
        return carry

    lax.fori_loop(0, NCH + len(stages) - 1, slot, 0)

    for i in range(3):
        x_copy(i).wait_recv()
    xf[...] = xo[...] + xr[0].astype(F32) + xr[1].astype(F32) + xr[2].astype(F32)
    for p in range(NZ):
        for k in range(4):
            lanes = (p % 2) * GRP + k * 128
            fs[k * TOK:(k + 1) * TOK, :] = xf[(p // 2) * TOK:(p // 2 + 1) * TOK, lanes:lanes + 128]
        v = fs[...]
        zsf[p] = v
        zs[p] = v.astype(ZTYPE)

    def z_copy(k):
        to = lax.rem(z + k, NZ)
        return copy(zs.at[to], zr.at[k], zz_s.at[k], zz_r.at[k], at(dz=k))

    for k in (4, 3, 5, 2, 6, 1, 7):
        z_copy(k).start()
    v = zsf[z]
    for k in (1, 7, 2, 6, 3, 5, 4):
        z_copy(k).wait_recv()
        v = v + zr[k].astype(F32)
    fs[...] = v
    for k in range(4):
        out[:, k * 128:(k + 1) * 128] = fs[k * TOK:(k + 1) * TOK, :].astype(BF16)

    for k in range(1, NZ):
        tz_copy(k).wait_send()
        z_copy(k).wait_send()
    for i in range(3):
        tx_copy(i).wait_send()
        x_copy(i).wait_send()

    @pl.when(primary)
    def _():
        copy(half_all, half_all, wo_s, wo_r, other_core).wait_send()
        down_own.wait_send()
        down_fwd.wait_send()
        for f in range(NF):
            weight_fwd(f).wait_send()

    @pl.when(jnp.logical_not(primary))
    def _():
        for f in range(NF):
            copy(wgu.at[f, mine], wgu.at[f, mine], wz_s.at[f], wz_r.at[f], z_partner).wait_send()
        down_z.wait_send()

    def drain(i, carry):
        for s in range(4):
            f = long_block(i, s)

            @pl.when(f != NF)
            def _():
                long_copy(i, s).wait_send()

            f = block(-turn(i) * s)

            @pl.when(f != NF)
            def _():
                gather_long(i, s, f).wait_send()

        for s in range(3):
            f = short_block(i, s)

            @pl.when(f != NF)
            def _():
                short_copy(i, s).wait_send()

            f = block(turn(i) * s)

            @pl.when(f != NF)
            def _():
                gather_short(i, s, f).wait_send()

        return carry

    lax.fori_loop(0, NCH, drain, 0)


def per_device(tokens, gate_weight, up_weight, down_weight):
    vmem, dma = pltpu.VMEM, pltpu.SemaphoreType.DMA
    scratch = [
        vmem((BLK, 128), F32),
        vmem((NZ, BLK, 128), BF16),
        vmem((BLK, 2 * GRP), F32),
        vmem((NCH, BLK, 2 * GRP), BF16),
        vmem((NF, 2 * GRP, 256), BF16),
        vmem((2, NF * 128, GRP), BF16),
        vmem((NCH, 3, 2 * BLK, 128), BF16),
        vmem((NCH, 2 * BLK, 128), F32),
        vmem((NCH, 2, 2 * BLK, 128), BF16),
        vmem((NCH, 2 * BLK, 128), F32),
        vmem((NCH, 3, 2 * BLK, 128), BF16),
        vmem((NCH, 2 * BLK, 128), F32),
        vmem((NCH, 2, 2 * BLK, 128), BF16),
        vmem((NCH, 2 * BLK, 128), F32),
        vmem((NCH, NF, BLK, 128), BF16),
        vmem((3, BLK, 2 * GRP), BF16),
        vmem((3, BLK, 2 * GRP), BF16),
        vmem((BLK, 2 * GRP), F32),
        vmem((NZ, BLK, 128), F32),
        vmem((NZ, BLK, 128), ZTYPE),
        vmem((NZ, BLK, 128), ZTYPE),
        dma((NZ,)), dma((NZ,)), dma((3,)), dma((3,)),
        dma, dma((NF,)), dma((NF,)), dma, dma, dma((NF,)), dma((NF,)),
        dma, dma, dma, dma, dma, dma, dma,
        dma((NCH, 4)), dma((NCH, 4)), dma((NCH, 3)), dma((NCH, 3)),
        dma((NCH, 4)), dma((NCH, 4)), dma((NCH, 3)), dma((NCH, 3)),
        dma((3,)), dma((3,)), dma((NZ,)), dma((NZ,)),
    ]
    return pl.pallas_call(
        kernel,
        out_shape=jax.ShapeDtypeStruct(tokens.shape, BF16),
        in_specs=[pl.BlockSpec(memory_space=pltpu.VMEM)] + [pl.BlockSpec(memory_space=pl.ANY)] * 3,
        out_specs=pl.BlockSpec(memory_space=pltpu.VMEM),
        scratch_shapes=scratch,
        compiler_params=pltpu.CompilerParams(
            collective_id=0, has_side_effects=True, vmem_limit_bytes=48 * 2**20
        ),
    )(tokens, gate_weight, up_weight, down_weight)


def solution(mesh):
    in_specs = (P("row", "col"), P("col", "row"), P("col", "row"), P("row", "col"))
    return jax.shard_map(
        per_device, mesh=mesh, in_specs=in_specs, out_specs=P("row", "col"), check_vma=False
    )
```

time: 403 us -> 105 us (0.26)
  the two profiles are of different devices: /device:TPU:23 before, /device:TPU:11 now
where the time goes in v1:
time: 105 us
  Pallas kernels  100 us (95%)
  local copies, waits for them, and re-layouts  4.93 us (5%)
    pallas_call x1, Pallas kernels, per_device(): pl.pallas_call(kernel, out_shape=jax.ShapeDtypeStruct(tokens.shape, BF16)...  100 us
    unnamed x9, local copies, waits for them, and re-layouts  4.93 us

profile of v1, /device:TPU:11, one launch (start us, length us, event | category | flops | bytes accessed | tf_op | source)
XLA Modules:
  0.0 105.2 jit_solution(3102072255411948189)
XLA Ops:
  0.0 0.0 copy-start
  0.0 1.2 %copy-done = bf16[512,896]{1,0:T(8,128)(2,1)S(1)} copy-done((bf16[512,896]{1,0:T(8,128)(2,1)S(1)}, bf16[512,896]{1,0:T(8,128)(2,1)}, u32[]{:S(2)}) %copy-start) | copy-done | bytes 917528
  1.2 0.0 copy-start.1
  1.2 1.2 %copy-done.1 = bf16[512,896]{1,0:T(8,128)(2,1)S(1)} copy-done((bf16[512,896]{1,0:T(8,128)(2,1)S(1)}, bf16[512,896]{1,0:T(8,128)(2,1)}, u32[]{:S(2)}) %copy-start.1) | copy-done | bytes 917528
  2.4 0.0 copy-start.2
  2.4 1.2 %copy-done.2 = bf16[896,512]{1,0:T(8,128)(2,1)S(1)} copy-done((bf16[896,512]{1,0:T(8,128)(2,1)S(1)}, bf16[896,512]{1,0:T(8,128)(2,1)}, u32[]{:S(2)}) %copy-start.2) | copy-done | bytes 917528
  3.5 0.0 copy-start.3
  3.5 0.8 copy-done.3
  4.3 100.3 %shard_map.46 = bf16[36,512]{1,0:T(8,128)(2,1)S(1)} custom-call(bf16[36,512]{1,0:T(8,128)(2,1)S(1)} %copy-done.3, bf16[512,896]{1,0:T(8,128)(2,1)S(1)} %copy-done, bf16[512,896]{1,0:T(8,128)(2,1)S(1)} %copy-done.1, bf16[896,512]{1,0:T(8,128)(2,1)S(1)} %copy-done.2), custom_call_target="tpu_custom_call" | custom-call | tf_op jit(solution)/shard_map/pallas_call | solution.py:430
  104.6 0.6 copy.6
Async XLA Ops:
  0.0 1.2 %copy-start = (bf16[512,896]{1,0:T(8,128)(2,1)S(1)}, bf16[512,896]{1,0:T(8,128)(2,1)}, u32[]{:S(2)}) copy-start(bf16[512,896]{1,0:T(8,128)(2,1)} %gate.1) | copy-start | bytes 2752516
  1.2 1.2 %copy-start.1 = (bf16[512,896]{1,0:T(8,128)(2,1)S(1)}, bf16[512,896]{1,0:T(8,128)(2,1)}, u32[]{:S(2)}) copy-start(bf16[512,896]{1,0:T(8,128)(2,1)} %up.1) | copy-start | bytes 2752516
  2.4 1.2 %copy-start.2 = (bf16[896,512]{1,0:T(8,128)(2,1)S(1)}, bf16[896,512]{1,0:T(8,128)(2,1)}, u32[]{:S(2)}) copy-start(bf16[896,512]{1,0:T(8,128)(2,1)} %down.1) | copy-start | bytes 2752516
  3.5 0.8 copy-start.3

commit v2 on v0

v2 whole, which is shorter than its diff:
```python
import functools

import jax
import jax.numpy as jnp
from jax import lax
from jax.experimental import pallas as pl
from jax.experimental.pallas import tpu as pltpu
from jax.sharding import PartitionSpec as P

F32, BF16 = jnp.float32, jnp.bfloat16
NX, NY, NZ = 4, 8, 8
TOK = 36
BLK = 144
GRP = 512
NF = 7
NCH = 4


def device(x, y, z, c):
    return {"row": (x * 4 + z // 2) * 2 + c, "col": lax.rem(z, 2) * 8 + y}


def kernel(
    tok, gate, up, down, out,
    tv, fs, tk, xf, tx, ws, ds, wgu, dw, msg_out, msg_in, hb, zsf, zs, zr,
    tl, tz_s, tz_r, tx_s, tx_r, wl, wz_s, wz_r, wo_s, wo_r, wf_s, wf_r, dl, dz_s, dz_r, do_s, do_r, df_s, df_r,
    ra_s, ra_r, ga_s, ga_r, zz_s, zz_r,
):
    row, col = lax.axis_index("row"), lax.axis_index("col")
    x, zh, c = row // 8, lax.rem(row // 2, 4), lax.rem(row, 2)
    zl, y = col // 8, lax.rem(col, 8)
    z = zh * 2 + zl
    primary = c == zl
    secondary = c != zl

    def at(dx=0, dy=0, dz=0):
        return device(lax.rem(x + dx + NX, NX), lax.rem(y + dy + NY, NY), lax.rem(z + dz + NZ, NZ), c)

    other_core = device(x, y, z, 1 - c)
    z_partner = device(x, y, zh * 2 + (1 - zl), c)
    xoff = lambda i: (2, 1, -1, 0)[i] if isinstance(i, int) else jnp.where(i == 0, 2, jnp.where(i == 1, 1, jnp.where(i == 2, -1, 0)))

    def copy(src, dst, send, recv, where):
        return pltpu.make_async_remote_copy(
            src_ref=src, dst_ref=dst, send_sem=send, recv_sem=recv,
            device_id=where, device_id_type=pl.DeviceIdType.MESH,
        )

    mine = pl.ds(pl.multiple_of(zl * GRP, GRP), GRP)
    theirs = pl.ds(pl.multiple_of((1 - zl) * GRP, GRP), GRP)
    cols = lambda f: pl.ds(pl.multiple_of(f * 128, 128), 128)

    def block(offset):
        return lax.rem(y + offset + NY, NY)

    bar = pltpu.get_barrier_semaphore()
    peers = [at(dz=k) for k in (4, 3, 5, 2, 6)] + [at(dx=2), at(dy=2), at(dy=-2)]
    peers += [at(dz=1), at(dz=-1), at(dx=1), at(dx=-1), at(dy=1), at(dy=-1), other_core]
    for p in peers:
        pl.semaphore_signal(bar, inc=1, device_id=p, device_id_type=pl.DeviceIdType.MESH)

    tokens = pltpu.make_async_copy(tok, tv, tl)
    tokens.start()

    @pl.when(primary)
    def _():
        for f in range(NF):
            pltpu.make_async_copy(gate.at[:, cols(f)], wgu.at[f, mine, pl.ds(0, 128)], wl).start()
            pltpu.make_async_copy(up.at[:, cols(f)], wgu.at[f, mine, pl.ds(128, 128)], wl).start()
        pltpu.make_async_copy(down, dw.at[zl], dl).start()

    @pl.when(secondary)
    def _():
        for f in range(NF):
            pltpu.make_async_copy(gate.at[:, cols(f)], ws.at[f, :, pl.ds(0, 128)], wl).start()
            pltpu.make_async_copy(up.at[:, cols(f)], ws.at[f, :, pl.ds(128, 128)], wl).start()
        pltpu.make_async_copy(down, ds, dl).start()

    tokens.wait()
    t = tv[...].astype(F32)
    for k in range(4):
        fs[k * TOK:(k + 1) * TOK, :] = t[:, k * 128:(k + 1) * 128]
    tk[3, z] = fs[...].astype(BF16)

    pl.semaphore_wait(bar, len(peers))

    def tz_copy(k):
        return copy(tk.at[3, z], tk.at[3, z], tz_s.at[k], tz_r.at[k], at(dz=k))

    def tx_copy(i, p):
        return copy(tk.at[3, p], tk.at[i, p], tx_s.at[i], tx_r.at[i], at(dx=-(2, 1, -1)[i]))

    for k in (1, 7, 2, 6, 3, 5, 4):
        tz_copy(k).start()
    for i in (1, 2):
        tx_copy(i, z).start()

    order = (4, 3, -3, 1, -1, 2, -2, 0)

    def weight_z(f):
        return copy(ws.at[f], wgu.at[f, mine], wz_s.at[f], wz_r.at[f], z_partner)

    def weight_own(f):
        return copy(wgu.at[f, mine], wgu.at[f, mine], wo_s, wo_r, other_core)

    def weight_fwd(f):
        return copy(wgu.at[f, theirs], wgu.at[f, theirs], wf_s.at[f], wf_r.at[f], other_core)

    down_z = copy(ds, dw.at[zl], dz_s, dz_r, z_partner)
    down_own = copy(dw.at[zl], dw.at[zl], do_s, do_r, other_core)
    down_fwd = copy(dw.at[1 - zl], dw.at[1 - zl], df_s, df_r, other_core)
    half_all = wgu.at[:, mine]

    def piece(k):
        src = lax.rem(z - k + NZ, NZ)
        copy(tk.at[3, src], tk.at[3, src], tz_s.at[k], tz_r.at[k], at(dz=k)).wait_recv()
        for i in (1, 2):
            tx_copy(i, src).start()

    def piece_far(k):
        tx_copy(0, lax.rem(z - k + NZ, NZ)).start()

    piece(1)
    piece(7)
    piece_far(0)

    @pl.when(secondary)
    def _():
        pltpu.make_async_copy(ws, ws, wl).wait()
        pltpu.make_async_copy(ds, ds, dl).wait()
        for o in order:
            f = block(o)

            @pl.when(f != NF)
            def _():
                weight_z(f).start()
        down_z.start()

    @pl.when(primary)
    def _():
        pltpu.make_async_copy(half_all, half_all, wl).wait()
        for f in range(NF):
            weight_own(f).start()
        pltpu.make_async_copy(ds, dw.at[zl], dl).wait()
        down_own.start()

    for ks, behind in (((2, 6), (1, 7)), ((3, 5), (2, 6)), ((4,), (3, 5, 4))):
        for k in ks:
            piece(k)
        for k in behind:
            piece_far(k)

    def assemble(i):
        for p in range(NZ):
            fs[...] = tk[i, p].astype(F32)
            for k in range(4):
                lanes = (p % 2) * GRP + k * 128
                xf[(p // 2) * TOK:(p // 2 + 1) * TOK, lanes:lanes + 128] = fs[k * TOK:(k + 1) * TOK, :]
        tx[i] = xf[...].astype(BF16)

    assemble(3)

    @pl.when(secondary)
    def _():
        copy(half_all, wgu.at[:, theirs], wo_s, wo_r, other_core).wait_recv()

    def turn(i):
        return 1 - 2 * (i % 2) if isinstance(i, int) else 1 - 2 * lax.rem(i, 2)

    def product(i, f):
        acc = jnp.dot(tx[i], wgu[f], preferred_element_type=F32)
        return jnp.concatenate([acc[:, :128], acc[:, 128:]], axis=0)

    def take_weights(*offsets):
        for o in offsets:
            f = block(o)

            @pl.when(jnp.logical_and(f != NF, primary))
            def _():
                copy(wgu.at[f, mine], wgu.at[f, theirs], wz_s.at[f], wz_r.at[f], z_partner).wait_recv()
                weight_fwd(f).start()

            @pl.when(jnp.logical_and(f != NF, secondary))
            def _():
                copy(wgu.at[f, mine], wgu.at[f, mine], wf_s.at[f], wf_r.at[f], other_core).wait_recv()

    def aside(i):
        return NF - 2 * i

    def unit(i, b):
        return jnp.where(b == NF, aside(i), b)

    def message(i, n, to):
        return copy(msg_out.at[n, i], msg_in.at[n, i], ra_s.at[i, n], ra_r.at[i, n], at(dy=turn(i) * to))

    MESSAGES = ((4, 2), (3, 1), (-3, -1), (1, 1), (-1, -1), (2, 2), (-2, -2))

    def send_term(i, n):
        b = block(turn(i) * MESSAGES[n][0])

        @pl.when(jnp.logical_and(b != NF, b != aside(i)))
        def _():
            msg_out[n, i] = product(i, b).astype(BF16)
            message(i, n, MESSAGES[n][1]).start()

    def send_term_moved(i):
        o = lax.rem(turn(i) * (NF - y) + NY, NY)
        n = jnp.where(o == 4, 0, jnp.where(o == 3, 1, jnp.where(o == 5, 2, jnp.where(o == 1, 3, 4))))
        to = jnp.where(o == 4, 2, jnp.where(o == 3, 1, jnp.where(o == 1, 1, -1)))

        @pl.when(jnp.logical_and(lax.rem(o + 2, 4) != 0, lax.rem(o + 8, 8) != 0))
        def _():
            @pl.when(aside(i) != NF)
            def _():
                msg_out[n, i] = product(i, aside(i)).astype(BF16)
                message(i, n, to).start()

    def send_sum(i, n, parts):
        b = block(turn(i) * MESSAGES[n][0])

        @pl.when(b != aside(i))
        def _():
            v = product(i, unit(i, b))
            for m in parts:
                message(i, m, MESSAGES[m][1]).wait_recv()
                v = v + msg_in[m, i].astype(F32)
            msg_out[n, i] = v.astype(BF16)
            message(i, n, MESSAGES[n][1]).start()

    def early(i, s):
        for n in ((0,), (1, 2), (3, 4))[s]:
            send_term(i, n)

    def tokens_of(i):
        copy(tk.at[3], tk.at[i], tx_s.at[i], tx_r.at[i], at(dx=-xoff(i))).wait_recv()
        assemble(i)

    def gather(i, n):
        d = turn(i)
        b, to = ((0, 1), (0, -1), (0, 2), (0, -2), (-2, 1), (-2, 2), (2, -1))[n]
        b = block(d * b)
        f = lax.rem(unit(i, b), NY)
        return b != aside(i), f, lambda: copy(hb.at[i, f], hb.at[i, f], ga_s.at[i, n], ga_r.at[i, n], at(dy=d * to))

    def gather_wait(i, n):
        b = block(turn(i) * (-1, 1, -2, 2, -3, -4, 3)[n])

        @pl.when(b != aside(i))
        def _():
            f = unit(i, b)
            copy(hb.at[i, f], hb.at[i, f], ga_s.at[i, n], ga_r.at[i, n], at(dy=turn(i))).wait_recv()

    def gather_start(i, n):
        ok, _, make = gather(i, n)

        @pl.when(ok)
        def _():
            make().start()

    def finish(i):
        @pl.when(y != aside(i))
        def _():
            f = unit(i, y)
            v = product(i, f)
            for n in (3, 4, 5, 6):
                message(i, n, 1).wait_recv()
                v = v + msg_in[n, i].astype(F32)
            g, u = v[:BLK], v[BLK:]
            hb[i, f] = (g / (1.0 + jnp.exp(-g)) * u).astype(BF16)
            for n in (2, 3, 0, 1):
                gather(i, n)[2]().start()

    def gather_on(i):
        gather_wait(i, 2)
        gather_start(i, 5)
        gather_start(i, 4)
        gather_wait(i, 3)
        gather_start(i, 6)

    def out_copy(i, k):
        src = zs.at[i, lax.rem(z + k, NZ)]
        return copy(src, zr.at[i, k], zz_s.at[i, k], zz_r.at[i, k], at(dx=xoff(i), dz=k))

    def project(i):
        for n in (0, 1, 4, 5, 6):
            gather_wait(i, n)

        @pl.when(i == 0)
        def _():
            @pl.when(primary)
            def _():
                copy(ds, dw.at[1 - zl], dz_s, dz_r, z_partner).wait_recv()
                down_fwd.start()

            @pl.when(secondary)
            def _():
                copy(ds, dw.at[zl], do_s, do_r, other_core).wait_recv()
                copy(ds, dw.at[1 - zl], df_s, df_r, other_core).wait_recv()

        h = jnp.concatenate([hb[i, f] for f in range(NF)], axis=1)
        for half in range(2):
            v = jnp.dot(h, dw[half], preferred_element_type=F32)
            xf[:, half * GRP:(half + 1) * GRP] = v
        for p in range(NZ):
            for k in range(4):
                lanes = (p % 2) * GRP + k * 128
                fs[k * TOK:(k + 1) * TOK, :] = xf[(p // 2) * TOK:(p // 2 + 1) * TOK, lanes:lanes + 128]
            v = fs[...]
            zs[i, p] = v.astype(BF16)

            @pl.when(i == 3)
            def _():
                zsf[p] = v

        for k in (4, 3, 5, 2, 6, 1, 7):
            out_copy(i, k).start()

        @pl.when(i != 3)
        def _():
            out_copy(i, 0).start()

    def over_chunks(body, low=0, high=NCH):
        def step(j, carry):
            body(j)
            return carry

        lax.fori_loop(low, high, step, 0)

    take_weights(4)
    early(3, 0)
    for i in (1, 2, 0):
        tokens_of(i)
    over_chunks(lambda j: early(j, 0), 0, 3)
    take_weights(3, -3)
    over_chunks(lambda j: early(j, 1))
    take_weights(1, -1)
    over_chunks(lambda j: early(j, 2))
    take_weights(2, -2, 0)
    over_chunks(send_term_moved, 1)

    def sums(i):
        send_sum(i, 5, (0, 1))
        send_sum(i, 6, (2,))

    stages = ((sums, 0), (finish, 1), (gather_on, 2), (project, 3))

    def slot(t, carry):
        for stage, s in stages:
            i = t - s

            @pl.when(jnp.logical_and(i >= 0, i < NCH))
            def _():
                stage(i)
        return carry

    lax.fori_loop(0, NCH + 3, slot, 0)

    def add(i, v):
        for k in (0, 1, 7, 2, 6, 3, 5, 4):
            if i != 3 or k > 0:
                out_copy(i, k).wait_recv()
                v = v + zr[i, k].astype(F32)
        return v

    v = zsf[z]
    for i in range(NCH):
        v = add(i, v)
    fs[...] = v
    for k in range(4):
        out[:, k * 128:(k + 1) * 128] = fs[k * TOK:(k + 1) * TOK, :].astype(BF16)

    for k in range(1, NZ):
        tz_copy(k).wait_send()
    for i in range(3):
        copy(tk.at[3], tk.at[i], tx_s.at[i], tx_r.at[i], at(dx=-(2, 1, -1)[i])).wait_send()
    for i in range(NCH):
        for k in range(i // 3, NZ):
            out_copy(i, k).wait_send()

    @pl.when(primary)
    def _():
        copy(half_all, half_all, wo_s, wo_r, other_core).wait_send()
        down_own.wait_send()
        down_fwd.wait_send()
        for f in range(NF):
            weight_fwd(f).wait_send()

    @pl.when(secondary)
    def _():
        for f in range(NF):
            copy(wgu.at[f, mine], wgu.at[f, mine], wz_s.at[f], wz_r.at[f], z_partner).wait_send()
        down_z.wait_send()

    def drain(i, carry):
        for n in range(7):
            b = block(turn(i) * MESSAGES[n][0])

            @pl.when(b != aside(i))
            def _():
                message(i, n, 1).wait_send()

            ok, _, make = gather(i, n)

            @pl.when(ok)
            def _():
                make().wait_send()

        return carry

    lax.fori_loop(0, NCH, drain, 0)


def per_device(tokens, gate_weight, up_weight, down_weight):
    vmem, dma = pltpu.VMEM, pltpu.SemaphoreType.DMA
    scratch = [
        vmem((TOK, GRP), BF16),
        vmem((BLK, 128), F32),
        vmem((NCH, NZ, BLK, 128), BF16),
        vmem((BLK, 2 * GRP), F32),
        vmem((NCH, BLK, 2 * GRP), BF16),
        vmem((NF, GRP, 256), BF16),
        vmem((NF * 128, GRP), BF16),
        vmem((NF, 2 * GRP, 256), BF16),
        vmem((2, NF * 128, GRP), BF16),
        vmem((7, NCH, 2 * BLK, 128), BF16),
        vmem((7, NCH, 2 * BLK, 128), BF16),
        vmem((NCH, NF, BLK, 128), BF16),
        vmem((NZ, BLK, 128), F32),
        vmem((NCH, NZ, BLK, 128), BF16),
        vmem((NCH, NZ, BLK, 128), BF16),
        dma, dma((NZ,)), dma((NZ,)), dma((3,)), dma((3,)),
        dma, dma((NF,)), dma((NF,)), dma, dma, dma((NF,)), dma((NF,)),
        dma, dma, dma, dma, dma, dma, dma,
        dma((NCH, 7)), dma((NCH, 7)), dma((NCH, 7)), dma((NCH, 7)),
        dma((NCH, NZ)), dma((NCH, NZ)),
    ]
    return pl.pallas_call(
        kernel,
        out_shape=jax.ShapeDtypeStruct(tokens.shape, BF16),
        in_specs=[pl.BlockSpec(memory_space=pl.ANY)] * 4,
        out_specs=pl.BlockSpec(memory_space=pltpu.VMEM),
        scratch_shapes=scratch,
        compiler_params=pltpu.CompilerParams(
            collective_id=0, has_side_effects=True, vmem_limit_bytes=63 * 2**20
        ),
    )(tokens, gate_weight, up_weight, down_weight)


def solution(mesh):
    in_specs = (P("row", "col"), P("col", "row"), P("col", "row"), P("row", "col"))
    return jax.shard_map(
        per_device, mesh=mesh, in_specs=in_specs, out_specs=P("row", "col"), check_vma=False
    )
```

time: 403 us -> 101 us (0.25)
  the two profiles are of different devices: /device:TPU:23 before, /device:TPU:1 now
where the time goes in v2:
time: 101 us
  Pallas kernels  99.9 us (99%)
  local copies, waits for them, and re-layouts  1.4 us (1%)
    pallas_call x1, Pallas kernels, per_device(): pl.pallas_call(kernel, out_shape=jax.ShapeDtypeStruct(tokens.shape, BF16)...  99.9 us

profile of v2, /device:TPU:1, one launch (start us, length us, event | category | flops | bytes accessed | tf_op | source)
XLA Modules:
  0.0 101.3 jit_solution(4440648777800933617)
XLA Ops:
  0.0 99.9 %shard_map.46 = bf16[36,512]{1,0:T(8,128)(2,1)} custom-call(bf16[36,512]{1,0:T(8,128)(2,1)} %tok.1, bf16[512,896]{1,0:T(8,128)(2,1)} %gate.1, bf16[512,896]{1,0:T(8,128)(2,1)} %up.1, bf16[896,512]{1,0:T(8,128)(2,1)} %down.1), custom_call_target="tpu_custom_call" | custom-call | tf_op jit(solution)/shard_map/pallas_call | solution.py:437
  99.9 1.4 %copy.6 = bf16[36,512]{1,0:T(8,128)(2,1)} copy(bf16[36,512]{1,0:T(8,128)(2,1)} %shard_map.46) | data formatting | bytes 73728

commit v3 on v2

--- a/solution.py
+++ b/solution.py
@@ -22,9 +22,9 @@
 
 def kernel(
     tok, gate, up, down, out,
-    tv, fs, tk, xf, tx, ws, ds, wgu, dw, msg_out, msg_in, hb, zsf, zs, zr,
+    tv, fs, tk, xf, tx, ws, ds, wgu, dw, msg_out, msg_in, hb, xs, xr, xo, zsf, zs, zr,
     tl, tz_s, tz_r, tx_s, tx_r, wl, wz_s, wz_r, wo_s, wo_r, wf_s, wf_r, dl, dz_s, dz_r, do_s, do_r, df_s, df_r,
-    ra_s, ra_r, ga_s, ga_r, zz_s, zz_r,
+    ra_s, ra_r, ga_s, ga_r, xx_s, xx_r, zz_s, zz_r,
 ):
     row, col = lax.axis_index("row"), lax.axis_index("col")
     x, zh, c = row // 8, lax.rem(row // 2, 4), lax.rem(row, 2)
@@ -90,26 +90,46 @@
     def tx_copy(i, p):
         return copy(tk.at[3, p], tk.at[i, p], tx_s.at[i], tx_r.at[i], at(dx=-(2, 1, -1)[i]))
 
+    order = (4, 3, -3, 1, -1, 2, -2, 0)
+
+    def weight_z(f):
+        return copy(ws.at[f], wgu.at[f, mine], wz_s.at[f], wz_r.at[f], z_partner)
+
+    def weight_own(f):
+        return copy(wgu.at[f, mine], wgu.at[f, mine], wo_s, wo_r, other_core)
+
+    def weight_fwd(f):
+        return copy(wgu.at[f, theirs], wgu.at[f, theirs], wf_s.at[f], wf_r.at[f], other_core)
+
+    down_z = copy(ds, dw.at[zl], dz_s, dz_r, z_partner)
+    down_own = copy(dw.at[zl], dw.at[zl], do_s, do_r, other_core)
+    down_fwd = copy(dw.at[1 - zl], dw.at[1 - zl], df_s, df_r, other_core)
+    half_all = wgu.at[:, mine]
+
     for k in (1, 7, 2, 6, 3, 5, 4):
         tz_copy(k).start()
     for i in (1, 2):
         tx_copy(i, z).start()
 
-    order = (4, 3, -3, 1, -1, 2, -2, 0)
-
-    def weight_z(f):
-        return copy(ws.at[f], wgu.at[f, mine], wz_s.at[f], wz_r.at[f], z_partner)
-
-    def weight_own(f):
-        return copy(wgu.at[f, mine], wgu.at[f, mine], wo_s, wo_r, other_core)
-
-    def weight_fwd(f):
-        return copy(wgu.at[f, theirs], wgu.at[f, theirs], wf_s.at[f], wf_r.at[f], other_core)
-
-    down_z = copy(ds, dw.at[zl], dz_s, dz_r, z_partner)
-    down_own = copy(dw.at[zl], dw.at[zl], do_s, do_r, other_core)
-    down_fwd = copy(dw.at[1 - zl], dw.at[1 - zl], df_s, df_r, other_core)
-    half_all = wgu.at[:, mine]
+    @pl.when(secondary)
+    def _():
+        pltpu.make_async_copy(ws, ws, wl).wait()
+        pltpu.make_async_copy(ds, ds, dl).wait()
+        for o in order:
+            f = block(o)
+
+            @pl.when(f != NF)
+            def _():
+                weight_z(f).start()
+        down_z.start()
+
+    @pl.when(primary)
+    def _():
+        pltpu.make_async_copy(half_all, half_all, wl).wait()
+        for f in range(NF):
+            weight_own(f).start()
+        pltpu.make_async_copy(ds, dw.at[zl], dl).wait()
+        down_own.start()
 
     def piece(k):
         src = lax.rem(z - k + NZ, NZ)
@@ -123,26 +143,6 @@
     piece(1)
     piece(7)
     piece_far(0)
-
-    @pl.when(secondary)
-    def _():
-        pltpu.make_async_copy(ws, ws, wl).wait()
-        pltpu.make_async_copy(ds, ds, dl).wait()
-        for o in order:
-            f = block(o)
-
-            @pl.when(f != NF)
-            def _():
-                weight_z(f).start()
-        down_z.start()
-
-    @pl.when(primary)
-    def _():
-        pltpu.make_async_copy(half_all, half_all, wl).wait()
-        for f in range(NF):
-            weight_own(f).start()
-        pltpu.make_async_copy(ds, dw.at[zl], dl).wait()
-        down_own.start()
 
     for ks, behind in (((2, 6), (1, 7)), ((3, 5), (2, 6)), ((4,), (3, 5, 4))):
         for k in ks:
@@ -193,7 +193,7 @@
     def message(i, n, to):
         return copy(msg_out.at[n, i], msg_in.at[n, i], ra_s.at[i, n], ra_r.at[i, n], at(dy=turn(i) * to))
 
-    MESSAGES = ((4, 2), (3, 1), (-3, -1), (1, 1), (-1, -1), (2, 2), (-2, -2))
+    MESSAGES = ((4, 1), (3, 1), (-3, -1), (1, 1), (-1, -1), (2, 2), (-2, -1))
 
     def send_term(i, n):
         b = block(turn(i) * MESSAGES[n][0])
@@ -205,15 +205,13 @@
 
     def send_term_moved(i):
         o = lax.rem(turn(i) * (NF - y) + NY, NY)
-        n = jnp.where(o == 4, 0, jnp.where(o == 3, 1, jnp.where(o == 5, 2, jnp.where(o == 1, 3, 4))))
-        to = jnp.where(o == 4, 2, jnp.where(o == 3, 1, jnp.where(o == 1, 1, -1)))
-
-        @pl.when(jnp.logical_and(lax.rem(o + 2, 4) != 0, lax.rem(o + 8, 8) != 0))
-        def _():
-            @pl.when(aside(i) != NF)
-            def _():
-                msg_out[n, i] = product(i, aside(i)).astype(BF16)
-                message(i, n, to).start()
+        n = jnp.where(o == 4, 0, jnp.where(o == 5, 2, jnp.where(o == 1, 3, 4)))
+        to = jnp.where((o == 4) | (o == 1), 1, -1)
+
+        @pl.when(((o == 4) | (o == 5) | (o == 1)) & (aside(i) != NF))
+        def _():
+            msg_out[n, i] = product(i, aside(i)).astype(BF16)
+            message(i, n, to).start()
 
     def send_sum(i, n, parts):
         b = block(turn(i) * MESSAGES[n][0])
@@ -228,7 +226,7 @@
             message(i, n, MESSAGES[n][1]).start()
 
     def early(i, s):
-        for n in ((0,), (1, 2), (3, 4))[s]:
+        for n in (0, 2, 3)[s:s + 1]:
             send_term(i, n)
 
     def tokens_of(i):
@@ -262,7 +260,7 @@
         def _():
             f = unit(i, y)
             v = product(i, f)
-            for n in (3, 4, 5, 6):
+            for n in (3, 4, 5):
                 message(i, n, 1).wait_recv()
                 v = v + msg_in[n, i].astype(F32)
             g, u = v[:BLK], v[BLK:]
@@ -277,9 +275,8 @@
         gather_wait(i, 3)
         gather_start(i, 6)
 
-    def out_copy(i, k):
-        src = zs.at[i, lax.rem(z + k, NZ)]
-        return copy(src, zr.at[i, k], zz_s.at[i, k], zz_r.at[i, k], at(dx=xoff(i), dz=k))
+    def x_copy(i):
+        return copy(xs.at[i], xr.at[i], xx_s.at[i], xx_r.at[i], at(dx=xoff(i)))
 
     def project(i):
         for n in (0, 1, 4, 5, 6):
@@ -301,23 +298,42 @@
         for half in range(2):
             v = jnp.dot(h, dw[half], preferred_element_type=F32)
             xf[:, half * GRP:(half + 1) * GRP] = v
+            lanes = slice(half * GRP, (half + 1) * GRP)
+
+
+        @pl.when((i == 1))
+        def _():
+            j = jnp.minimum(i, 2)
+            xs[j] = xf[...].astype(BF16)
+            x_copy(j).start()
+
+        @pl.when((i == 0) | (i == 2))
+        def _():
+            j = jnp.minimum(i, 2)
+            split(lambda p, v: put(zs, j, p, v))
+            for k in (4, 3, 5, 2, 6, 0, 1, 7):
+                z_copy(j, k).start()
+
+        @pl.when(i == 3)
+        def _():
+            xo[...] = xf[...]
+
+    def split(store):
         for p in range(NZ):
             for k in range(4):
                 lanes = (p % 2) * GRP + k * 128
                 fs[k * TOK:(k + 1) * TOK, :] = xf[(p // 2) * TOK:(p // 2 + 1) * TOK, lanes:lanes + 128]
-            v = fs[...]
-            zs[i, p] = v.astype(BF16)
-
-            @pl.when(i == 3)
-            def _():
-                zsf[p] = v
-
-        for k in (4, 3, 5, 2, 6, 1, 7):
-            out_copy(i, k).start()
-
-        @pl.when(i != 3)
-        def _():
-            out_copy(i, 0).start()
+            store(p, fs[...])
+
+    def put(ref, j, p, v):
+        ref[j, p] = v.astype(BF16)
+
+    def put_own(p, v):
+        zsf[p] = v
+        zs[3, p] = v.astype(BF16)
+
+    def z_copy(i, k):
+        return copy(zs.at[i, lax.rem(z + k, NZ)], zr.at[i, k], zz_s.at[i, k], zz_r.at[i, k], at(dx=xoff(i), dz=k))
 
     def over_chunks(body, low=0, high=NCH):
         def step(j, carry):
@@ -338,9 +354,15 @@
     take_weights(2, -2, 0)
     over_chunks(send_term_moved, 1)
 
+    def first_sums(i):
+        send_sum(i, 1, (0,))
+        send_sum(i, 6, (2,))
+
     def sums(i):
-        send_sum(i, 5, (0, 1))
-        send_sum(i, 6, (2,))
+        send_sum(i, 5, (1,))
+        send_sum(i, 4, (6,))
+
+    over_chunks(first_sums)
 
     stages = ((sums, 0), (finish, 1), (gather_on, 2), (project, 3))
 
@@ -355,27 +377,34 @@
 
     lax.fori_loop(0, NCH + 3, slot, 0)
 
-    def add(i, v):
+    v = xo[...]
+    for i in (1,):
+        x_copy(i).wait_recv()
+        v = v + xr[i].astype(F32)
+    xf[...] = v
+    split(put_own)
+    for k in (4, 3, 5, 2, 6, 1, 7):
+        z_copy(3, k).start()
+    v = zsf[z]
+    for i in (0, 2, 3):
         for k in (0, 1, 7, 2, 6, 3, 5, 4):
             if i != 3 or k > 0:
-                out_copy(i, k).wait_recv()
+                z_copy(i, k).wait_recv()
                 v = v + zr[i, k].astype(F32)
-        return v
-
-    v = zsf[z]
-    for i in range(NCH):
-        v = add(i, v)
     fs[...] = v
     for k in range(4):
         out[:, k * 128:(k + 1) * 128] = fs[k * TOK:(k + 1) * TOK, :].astype(BF16)
 
     for k in range(1, NZ):
         tz_copy(k).wait_send()
+        z_copy(3, k).wait_send()
     for i in range(3):
         copy(tk.at[3], tk.at[i], tx_s.at[i], tx_r.at[i], at(dx=-(2, 1, -1)[i])).wait_send()
-    for i in range(NCH):
-        for k in range(i // 3, NZ):
-            out_copy(i, k).wait_send()
+    for i in (1,):
+        x_copy(i).wait_send()
+    for i in (0, 2):
+        for k in range(NZ):
+            z_copy(i, k).wait_send()
 
     @pl.when(primary)
     def _():
@@ -425,6 +454,9 @@
         vmem((7, NCH, 2 * BLK, 128), BF16),
         vmem((7, NCH, 2 * BLK, 128), BF16),
         vmem((NCH, NF, BLK, 128), BF16),
+        vmem((3, BLK, 2 * GRP), BF16),
+        vmem((3, BLK, 2 * GRP), BF16),
+        vmem((BLK, 2 * GRP), F32),
         vmem((NZ, BLK, 128), F32),
         vmem((NCH, NZ, BLK, 128), BF16),
         vmem((NCH, NZ, BLK, 128), BF16),
@@ -432,7 +464,7 @@
         dma, dma((NF,)), dma((NF,)), dma, dma, dma((NF,)), dma((NF,)),
         dma, dma, dma, dma, dma, dma, dma,
         dma((NCH, 7)), dma((NCH, 7)), dma((NCH, 7)), dma((NCH, 7)),
-        dma((NCH, NZ)), dma((NCH, NZ)),
+        dma((3,)), dma((3,)), dma((NCH, NZ)), dma((NCH, NZ)),
     ]
     return pl.pallas_call(
         kernel,

time: 101 us -> 94.8 us (0.939)
  Pallas kernels: 99.9 us -> 93.2 us
    pallas_call x1, Pallas kernels: 99.9 us -> 93.2 us  [per_device(): pl.pallas_call(kernel, out_shape=jax.ShapeDtypeStruct(tokens.shape, BF16)...]
where the time goes in v3:
time: 94.8 us; the launch traced here: 94.6 us
  Pallas kernels  93.2 us (98%)
  local copies, waits for them, and re-layouts  1.4 us (1%)
    pallas_call x1, Pallas kernels, per_device(): pl.pallas_call(kernel, out_shape=jax.ShapeDtypeStruct(tokens.shape, BF16)...  93.2 us

profile of v3, /device:TPU:1, one launch (start us, length us, event | category | flops | bytes accessed | tf_op | source)
XLA Modules:
  0.0 94.6 jit_solution(15523219379354594684)
XLA Ops:
  0.0 93.2 %shard_map.46 = bf16[36,512]{1,0:T(8,128)(2,1)} custom-call(bf16[36,512]{1,0:T(8,128)(2,1)} %tok.1, bf16[512,896]{1,0:T(8,128)(2,1)} %gate.1, bf16[512,896]{1,0:T(8,128)(2,1)} %up.1, bf16[896,512]{1,0:T(8,128)(2,1)} %down.1), custom_call_target="tpu_custom_call" | custom-call | tf_op jit(solution)/shard_map/pallas_call | solution.py:469
  93.2 1.4 %copy.6 = bf16[36,512]{1,0:T(8,128)(2,1)} copy(bf16[36,512]{1,0:T(8,128)(2,1)} %shard_map.46) | data formatting | bytes 73728

commit v4 on v3

--- a/solution.py
+++ b/solution.py
@@ -193,7 +193,7 @@
     def message(i, n, to):
         return copy(msg_out.at[n, i], msg_in.at[n, i], ra_s.at[i, n], ra_r.at[i, n], at(dy=turn(i) * to))
 
-    MESSAGES = ((4, 1), (3, 1), (-3, -1), (1, 1), (-1, -1), (2, 2), (-2, -1))
+    MESSAGES = ((4, 2), (3, 1), (-3, -1), (1, 1), (-1, -1), (2, 2), (-2, -2))
 
     def send_term(i, n):
         b = block(turn(i) * MESSAGES[n][0])
@@ -205,13 +205,15 @@
 
     def send_term_moved(i):
         o = lax.rem(turn(i) * (NF - y) + NY, NY)
-        n = jnp.where(o == 4, 0, jnp.where(o == 5, 2, jnp.where(o == 1, 3, 4)))
-        to = jnp.where((o == 4) | (o == 1), 1, -1)
-
-        @pl.when(((o == 4) | (o == 5) | (o == 1)) & (aside(i) != NF))
-        def _():
-            msg_out[n, i] = product(i, aside(i)).astype(BF16)
-            message(i, n, to).start()
+        n = jnp.where(o == 4, 0, jnp.where(o == 3, 1, jnp.where(o == 5, 2, jnp.where(o == 1, 3, 4))))
+        to = jnp.where(o == 4, 2, jnp.where(o == 3, 1, jnp.where(o == 1, 1, -1)))
+
+        @pl.when(jnp.logical_and(lax.rem(o + 2, 4) != 0, lax.rem(o + 8, 8) != 0))
+        def _():
+            @pl.when(aside(i) != NF)
+            def _():
+                msg_out[n, i] = product(i, aside(i)).astype(BF16)
+                message(i, n, to).start()
 
     def send_sum(i, n, parts):
         b = block(turn(i) * MESSAGES[n][0])
@@ -226,7 +228,7 @@
             message(i, n, MESSAGES[n][1]).start()
 
     def early(i, s):
-        for n in (0, 2, 3)[s:s + 1]:
+        for n in ((0,), (1, 2), (3, 4))[s]:
             send_term(i, n)
 
     def tokens_of(i):
@@ -260,7 +262,7 @@
         def _():
             f = unit(i, y)
             v = product(i, f)
-            for n in (3, 4, 5):
+            for n in (3, 4, 5, 6):
                 message(i, n, 1).wait_recv()
                 v = v + msg_in[n, i].astype(F32)
             g, u = v[:BLK], v[BLK:]
@@ -301,15 +303,15 @@
             lanes = slice(half * GRP, (half + 1) * GRP)
 
 
-        @pl.when((i == 1))
+        @pl.when((i == 0) | (i == 1))
         def _():
             j = jnp.minimum(i, 2)
             xs[j] = xf[...].astype(BF16)
             x_copy(j).start()
 
-        @pl.when((i == 0) | (i == 2))
-        def _():
-            j = jnp.minimum(i, 2)
+        @pl.when((i == 2))
+        def _():
+            j = 2
             split(lambda p, v: put(zs, j, p, v))
             for k in (4, 3, 5, 2, 6, 0, 1, 7):
                 z_copy(j, k).start()
@@ -354,15 +356,9 @@
     take_weights(2, -2, 0)
     over_chunks(send_term_moved, 1)
 
-    def first_sums(i):
-        send_sum(i, 1, (0,))
+    def sums(i):
+        send_sum(i, 5, (0, 1))
         send_sum(i, 6, (2,))
-
-    def sums(i):
-        send_sum(i, 5, (1,))
-        send_sum(i, 4, (6,))
-
-    over_chunks(first_sums)
 
     stages = ((sums, 0), (finish, 1), (gather_on, 2), (project, 3))
 
@@ -378,7 +374,7 @@
     lax.fori_loop(0, NCH + 3, slot, 0)
 
     v = xo[...]
-    for i in (1,):
+    for i in (0, 1):
         x_copy(i).wait_recv()
         v = v + xr[i].astype(F32)
     xf[...] = v
@@ -386,7 +382,7 @@
     for k in (4, 3, 5, 2, 6, 1, 7):
         z_copy(3, k).start()
     v = zsf[z]
-    for i in (0, 2, 3):
+    for i in (2, 3):
         for k in (0, 1, 7, 2, 6, 3, 5, 4):
             if i != 3 or k > 0:
                 z_copy(i, k).wait_recv()
@@ -400,9 +396,9 @@
         z_copy(3, k).wait_send()
     for i in range(3):
         copy(tk.at[3], tk.at[i], tx_s.at[i], tx_r.at[i], at(dx=-(2, 1, -1)[i])).wait_send()
-    for i in (1,):
+    for i in (0, 1):
         x_copy(i).wait_send()
-    for i in (0, 2):
+    for i in (2,):
         for k in range(NZ):
             z_copy(i, k).wait_send()
 

time: 94.8 us -> 96.9 us (1.022)
  Pallas kernels: 93.2 us -> 95.3 us
    pallas_call x1, Pallas kernels: 93.2 us -> 95.3 us  [per_device(): pl.pallas_call(kernel, out_shape=jax.ShapeDtypeStruct(tokens.shape, BF16)...]
where the time goes in v4:
time: 96.9 us; the launch traced here: 96.7 us
  Pallas kernels  95.3 us (98%)
  local copies, waits for them, and re-layouts  1.4 us (1%)
    pallas_call x1, Pallas kernels, per_device(): pl.pallas_call(kernel, out_shape=jax.ShapeDtypeStruct(tokens.shape, BF16)...  95.3 us

profile of v4, /device:TPU:1, one launch (start us, length us, event | category | flops | bytes accessed | tf_op | source)
XLA Modules:
  0.0 96.7 jit_solution(15640762466231510731)
XLA Ops:
  0.0 95.3 %shard_map.46 = bf16[36,512]{1,0:T(8,128)(2,1)} custom-call(bf16[36,512]{1,0:T(8,128)(2,1)} %tok.1, bf16[512,896]{1,0:T(8,128)(2,1)} %gate.1, bf16[512,896]{1,0:T(8,128)(2,1)} %up.1, bf16[896,512]{1,0:T(8,128)(2,1)} %down.1), custom_call_target="tpu_custom_call" | custom-call | tf_op jit(solution)/shard_map/pallas_call | solution.py:465
  95.3 1.4 %copy.6 = bf16[36,512]{1,0:T(8,128)(2,1)} copy(bf16[36,512]{1,0:T(8,128)(2,1)} %shard_map.46) | data formatting | bytes 73728
